TPU v7x, 512 devices: a whole 4x8x8 slice. The times are simulated.
512 devices in a mesh: vocab: 64 (over z, y), inner: 2 (over core), rep: 4 (over x).
Axes of the slice: x: 4, y: 8, z: 8, core: 2. Of those that a mesh axis runs over, the one named last changes fastest.
Arguments:
- teacher_hidden: bfloat16 [512, 4608], P('rep', 'inner'), may hold values from -6 to 6
- teacher_embed: bfloat16 [131072, 4608], P(('vocab', 'rep'), 'inner'), may hold values from -0.87890625 to 0.87890625
- student_hidden: bfloat16 [512, 3584], P('rep', 'inner'), may hold values from -6 to 6
- student_embed: bfloat16 [131072, 3584], P(('vocab', 'rep'), 'inner'), may hold values from -1 to 1
- labels: int32 [512], replicated, may hold values from 0 to 131071, as said below
- loss_mask: int32 [512], replicated, may hold values 0 or 1
Outputs:
- loss: float32 [], replicated
- hidden_grad: bfloat16 [512, 3584], P('rep', 'inner')
Inputs may be any that keep to these rules, and one draw needn't show every extreme that they name: `labels`: split the tokens into quarters of 128 rows in order, and the vocabulary into blocks of 512 entries numbered vocab index times 4 plus rep index. The ids of the tokens of quarter r lie only in blocks with rep index r, and every vocab index has at least one token of the quarter whose id lies in its block.
All inputs are finite; a program needn't handle non-finite values.
Results may differ from a plain program's by a relative error of at most 0.009.
Values may be sent and summed in bfloat16 or wider, within the bound.
A program may use at most 64 MiB of HBM per device.

v0:
```python
import jax
import jax.numpy as jnp
from jax import lax
from jax.sharding import PartitionSpec as P

LOGIT_CAP = 30.0
SOFTMAX_TEMPER = 2.0
SOFT_LOSS_WEIGHT = 0.5


def capped(scores):
    bounded = jnp.tanh(scores / LOGIT_CAP)
    return (LOGIT_CAP * bounded, bounded)


def against_rows(left, table):
    return lax.dot_general(
        left, table, (((1,), (1,)), ((), ())), preferred_element_type=jnp.float32
    )


def shards(teacher_hidden, teacher_embed, student_hidden, student_embed, labels, loss_mask):
    tokens = labels.shape[0]
    half_rows = tokens // lax.axis_size("inner")
    first_row = lax.axis_index("inner") * half_rows
    shard_rows = student_embed.shape[0]
    rep_count = lax.axis_size("rep")
    teacher_part = against_rows(
        lax.all_gather(teacher_hidden, "rep", axis=0, tiled=True), teacher_embed
    )
    teacher_scores = lax.psum_scatter(
        teacher_part.astype(jnp.bfloat16), "inner", scatter_dimension=0, tiled=True
    ).astype(jnp.float32)
    teacher_logit_rows = capped(teacher_scores)[0]
    teacher_probability = jnp.exp(teacher_logit_rows / SOFTMAX_TEMPER).astype(jnp.bfloat16)
    teacher_exp_values = lax.optimization_barrier(teacher_probability).astype(jnp.float32)
    student_part = against_rows(
        lax.all_gather(student_hidden, "rep", axis=0, tiled=True), student_embed
    )
    student_scores = lax.psum_scatter(student_part, "inner", scatter_dimension=0, tiled=True)
    student_logit_rows, bounded = capped(student_scores)
    soft_loss_terms = jnp.exp(student_logit_rows / SOFTMAX_TEMPER)
    hard_loss_terms = jnp.exp(student_logit_rows)
    offset = (lax.axis_index("vocab") * rep_count + lax.axis_index("rep")) * shard_rows
    columns = offset + jnp.arange(shard_rows, dtype=jnp.int32)
    own_labels = lax.dynamic_slice_in_dim(labels, first_row, half_rows, 0)
    target_labels = (columns[None, :] == own_labels[:, None]).astype(jnp.float32)
    soft_part = jnp.sum(soft_loss_terms, axis=1)
    hard_part = jnp.sum(hard_loss_terms, axis=1)
    cross_part = jnp.sum(teacher_exp_values * student_logit_rows, axis=1)
    label_part = jnp.sum(target_labels * student_logit_rows, axis=1)
    teacher_partition, soft_loss_total, hard_loss_total, cross_entropy_sum, label_logit_value = (
        lax.psum(
            (jnp.sum(teacher_exp_values, axis=1), soft_part, hard_part, cross_part, label_part),
            ("vocab", "rep"),
        )
    )
    cross_entropy = cross_entropy_sum / SOFTMAX_TEMPER
    weight_matrix = lax.dynamic_slice_in_dim(loss_mask, first_row, half_rows, 0).astype(jnp.float32)
    token_losses = SOFT_LOSS_WEIGHT * SOFTMAX_TEMPER * SOFTMAX_TEMPER * (
        jnp.log(soft_loss_total) - cross_entropy / teacher_partition
    ) + (1.0 - SOFT_LOSS_WEIGHT) * (jnp.log(hard_loss_total) - label_logit_value)
    loss_sum = lax.psum(jnp.sum(weight_matrix * token_losses), "inner")
    loss = loss_sum / jnp.maximum(jnp.sum(loss_mask.astype(jnp.float32)), 1.0)
    capped_slope = weight_matrix[:, None] * (
        SOFT_LOSS_WEIGHT
        * SOFTMAX_TEMPER
        * (
            soft_loss_terms / soft_loss_total[:, None]
            - teacher_exp_values / teacher_partition[:, None]
        )
        + (1.0 - SOFT_LOSS_WEIGHT) * (hard_loss_terms / hard_loss_total[:, None] - target_labels)
    )
    logit_grad = (capped_slope * (1.0 - bounded * bounded)).astype(jnp.bfloat16)
    grad_all = lax.all_gather(logit_grad, "inner", axis=0, tiled=True)
    own_rows = tokens // rep_count
    full_grad = jnp.dot(grad_all, student_embed, preferred_element_type=jnp.float32)
    summed = lax.psum(full_grad, ("vocab", "rep"))
    hidden_grad = lax.dynamic_slice_in_dim(
        summed, lax.axis_index("rep") * own_rows, own_rows, 0
    ).astype(jnp.bfloat16)
    return (loss, hidden_grad)


def solution(mesh):
    placed = (
        P("rep", "inner"),
        P(("vocab", "rep"), "inner"),
        P("rep", "inner"),
        P(("vocab", "rep"), "inner"),
        P(),
        P(),
    )
    return jax.shard_map(
        shards, mesh=mesh, in_specs=placed, out_specs=(P(), P("rep", "inner")), check_vma=False
    )
```

profile of v0, /device:TPU:1, one launch (start us, length us, event | category | flops | bytes accessed | tf_op | source)
XLA Modules:
  0.0 2243.6 jit_solution(15865800025442499931)
XLA Ops:
  7.2 0.0 copy-start
  7.2 0.0 all-gather.5.cloned.1.call-start
  7.2 0.7 all-gather.5.cloned.1.call-update
  7.9 0.0 all-gather.3.cloned.1.call-start
  8.0 0.7 all-gather.3.cloned.1.call-update
  8.7 0.0 reduce-scatter.5.cloned.1.call-start
  8.7 45.3 %all-gather.5.cloned.1.call-done = bf16[512,2304]{1,0:T(8,128)(2,1)} async-done(((bf16[128,2304]{1,0:T(8,128)(2,1)}), bf16[512,2304]{1,0:T(8,128)(2,1)}) %all-gather.5.cloned.1.call-update) | async-done | bytes 2359312 | tf_op jit(solution)/shard_map/all_gather | solution.py:29
  54.0 0.0 copy-done
  54.0 3.9 convolution_convert_fusion
  57.8 0.0 reduce-scatter.5.cloned.1.call-update
  57.9 0.0 copy-start.3
  57.9 0.0 copy-start.2
  57.9 0.0 reduce-scatter.3.cloned.1.call-start
  57.9 32.3 %all-gather.3.cloned.1.call-done = bf16[512,1792]{1,0:T(8,128)(2,1)} async-done(((bf16[128,1792]{1,0:T(8,128)(2,1)}), bf16[512,1792]{1,0:T(8,128)(2,1)}) %all-gather.3.cloned.1.call-update) | async-done | bytes 1835024 | tf_op jit(solution)/shard_map/all_gather | solution.py:38
  90.2 4.2 fusion.10
  94.4 0.0 reduce-scatter.3.cloned.1.call-update
  94.5 0.0 copy-done.3
  94.5 0.1 dynamic_slice.10
  94.5 0.0 copy-done.2
  94.5 0.1 dynamic-slice_convert_fusion.1
  94.6 0.6 convert_reduce_fusion.1
  95.2 15.4 reduce-scatter.5.cloned.1.call-done
  110.6 1.1 exponential_convert_fusion
  111.7 19.8 reduce-scatter.3.cloned.1.call-done
  131.5 1.6 fusion.9
  133.0 579.8 %all-reduce.1 = (f32[256]{0:T(256)S(1)}, f32[256]{0:T(256)S(1)}, f32[256]{0:T(256)S(1)}) all-reduce(f32[256]{0:T(256)S(1)} %get-tuple-element.5, f32[256]{0:T(256)S(1)} %get-tuple-element.6, f32[256]{0:T(256)S(1)} %get-tuple-element.2), channel_id=1, replica_groups=mesh['vocab'=64,'inner'=2,'rep'=4] {'vocab','rep'}, use_global_device_ids=true, to_apply=%region_9.0 | all-reduce | flops 768 | bytes 6144 | tf_op jit(solution)/shard_map/psum | solution.py:53
  712.8 0.0 copy-start.1
  712.8 1.6 fusion.6
  714.4 112.6 %all_gather.11 = bf16[512,512]{1,0:T(8,128)(2,1)S(1)} all-gather(bf16[256,512]{1,0:T(8,128)(2,1)S(1)} %fusion.6), channel_id=1, replica_groups=mesh['vocab'=64,'inner'=2,'rep'=4] {'inner'}, dimensions={0}, use_global_device_ids=true | all-gather | bytes 786432 | tf_op jit(solution)/shard_map/all_gather | solution.py:75
  827.0 0.0 copy-done.1
  827.0 2.9 fusion.11
  829.9 1180.7 %all-reduce.3 = (f32[256]{0:T(256)S(1)}, f32[256]{0:T(256)S(1)}, bf16[512,1792]{1,0:T(8,128)(2,1)}) all-reduce(f32[256]{0:T(256)S(1)} %get-tuple-element.4, f32[256]{0:T(256)S(1)} %get-tuple-element.3, f32[512,1792]{1,0:T(8,128)} %fusion.11), channel_id=1, replica_groups=mesh['vocab'=64,'inner'=2,'rep'=4] {'vocab','rep'}, use_global_device_ids=true, to_apply=%region_11.0 | all-reduce | flops 918016 | bytes 5509120 | tf_op jit(solution)/shard_map/psum | solution.py:53
  2010.5 0.7 multiply_reduce_fusion
  2011.9 221.6 %psum.54 = f32[]{:T(128)} all-reduce(f32[]{:T(128)} %multiply_reduce_fusion), channel_id=1, replica_groups=mesh['vocab'=64,'inner'=2,'rep'=4] {'inner'}, use_global_device_ids=true, to_apply=%region_13.0 | all-reduce | flops 1 | bytes 8 | tf_op jit(solution)/shard_map/psum | solution.py:63
  2233.5 1.8 dynamic-slice_convert_fusion
  (1 shorter events, 0.0 us)
Async XLA Ops:
  7.2 46.8 %copy-start = (bf16[512,2304]{1,0:T(8,128)(2,1)S(1)}, bf16[512,2304]{1,0:T(8,128)(2,1)}, u32[]{:S(2)}) copy-start(bf16[512,2304]{1,0:T(8,128)(2,1)} %param.7) | copy-start | bytes 7077892
  7.2 46.8 %all-gather.5.cloned.1.call-start = ((), (), s32[]{:S(2)}) async-start(), calls=%async_computation.4 | async-start | bytes 2949120 | tf_op jit(solution)/shard_map/all_gather | solution.py:29
  7.9 82.3 %all-gather.3.cloned.1.call-start = ((), (), s32[]{:S(2)}) async-start(), calls=%async_computation.2 | async-start | bytes 2293760 | tf_op jit(solution)/shard_map/all_gather | solution.py:38
  8.7 101.9 %reduce-scatter.5.cloned.1.call-start = ((), (), s32[]{:S(2)}) async-start(), calls=%async_computation.5 | async-start | bytes 786432 | tf_op jit(solution)/shard_map/reduce_scatter | solution.py:31
  57.9 36.6 %copy-start.3 = (s32[512]{0:T(512)S(1)}, s32[512]{0:T(512)}, u32[]{:S(2)}) copy-start(s32[512]{0:T(512)} %param.10) | copy-start | bytes 6148
  57.9 36.7 %copy-start.2 = (s32[512]{0:T(512)S(1)}, s32[512]{0:T(512)}, u32[]{:S(2)}) copy-start(s32[512]{0:T(512)} %param.11) | copy-start | bytes 6148
  57.9 73.6 %reduce-scatter.3.cloned.1.call-start = ((), (), s32[]{:S(2)}) async-start(), calls=%async_computation.3 | async-start | bytes 1572864 | tf_op jit(solution)/shard_map/reduce_scatter | solution.py:40
  712.8 114.2 %copy-start.1 = (bf16[512,1792]{1,0:T(8,128)(2,1)S(1)}, bf16[512,1792]{1,0:T(8,128)(2,1)}, u32[]{:S(2)}) copy-start(bf16[512,1792]{1,0:T(8,128)(2,1)} %param.9) | copy-start | bytes 5505028
Sparse Core Ops, SparseCore 0:
  10.1 43.8 all-gather.4
  56.1 34.1 all-gather.2
  93.0 17.5 reduce-scatter.4
  113.5 17.9 reduce-scatter.2
where the time goes:
time: 2240 us
  blocking collectives  2090 us (93%)
  waiting for transfers between devices  114 us (5%)
    psum x2, blocking collectives, shards(): lax.psum((jnp.sum(teacher_exp_values, axis=1), soft_part, hard_part, cros...  1760 us
    psum x1, blocking collectives, shards(): loss_sum = lax.psum(jnp.sum(weight_matrix * token_losses), 'inner')  222 us
    all_gather x1, blocking collectives, shards(): grad_all = lax.all_gather(logit_grad, 'inner', axis=0, tiled=True)  113 us
    all_gather x1, waiting for transfers between devices, shards(): lax.all_gather(teacher_hidden, 'rep', axis=0, tiled=True)  45.3 us
  transfers between devices with their start and end apart: 4, of which 4 were waited for; matrix products, arithmetic and copies ran while one was open for 0% of the time, Pallas kernels for 0%

commit v1 on v0

v1 whole, which is shorter than its diff:
```python
import jax
import jax.numpy as jnp
from jax import lax
from jax.experimental import pallas as pl
from jax.experimental.pallas import tpu as pltpu
from jax.sharding import PartitionSpec as P

MESH = pl.DeviceIdType.MESH
CAP = 30.0
NX, NY, NZ = 4, 8, 8
TOK, DT, DS, VB = 512, 2304, 1792, 512
HALF = TOK // 2
QUARTER = TOK // NX
CXY, CYX = 512, 384
CA = CXY + CYX
F32, BF16 = jnp.float32, jnp.bfloat16


def nt(left, right):
    return lax.dot_general(left, right, (((1,), (1,)), ((), ())), preferred_element_type=F32)


def body(
    th, te, sh, se, lab, msk, loss_ref, out_ref,
    thg, shg, tev, sev,
    tsend, trecv, town, ssend, srecv, sown,
    wts, soft, bnd, labc, mskc, stat, statc, sx, sy, sz, lbuf, lrecv,
    gfull, gx, gy, gz, rx, ry, rz, hxy, hxz, r2y, r2z, hx2, r2x, a3, b3, ra, rb, outv,
    lsem, gs, gr, cs, cr, xs, xr, ys, yr, zs, zr, x1s, x1r, y1s, y1r, z1s, z1r,
    x2s, x2r, y2s, y2r, z2s, z2r, az, azr, by, byr, ay, ayr, bz, bzr,
):
    v = lax.axis_index("vocab")
    c = lax.axis_index("inner")
    x = lax.axis_index("rep")
    z, y = v // NY, v % NY

    def xi(k):
        return lax.rem(x + k, NX)

    def yi(k):
        return lax.rem(y + k, NY)

    def zi(k):
        return lax.rem(z + k, NZ)

    def xp(k):
        return (v, c, xi(k))

    def yp(k):
        return (z * NY + yi(k), c, x)

    def zp(k):
        return (zi(k) * NY + y, c, x)

    cp = (v, 1 - c, x)

    def send(src, dst, ssem, rsem, to):
        copy = pltpu.make_async_remote_copy(
            src_ref=src, dst_ref=dst, send_sem=ssem, recv_sem=rsem, device_id=to, device_id_type=MESH
        )
        copy.start()
        return copy

    def arrive(copies):
        for copy in copies:
            copy.wait_recv()

    def leave(copies):
        for copy in copies:
            copy.wait_send()

    loads = [
        pltpu.make_async_copy(se, sev, lsem.at[0]),
        pltpu.make_async_copy(te, tev, lsem.at[1]),
        pltpu.make_async_copy(sh, shg.at[x], lsem.at[2]),
        pltpu.make_async_copy(th, thg.at[x], lsem.at[3]),
    ]
    for load in loads:
        load.start()

    barrier = pltpu.get_barrier_semaphore()
    for k in range(1, NX):
        pl.semaphore_signal(barrier, inc=1, device_id=xp(k), device_id_type=MESH)
    for k in range(1, NY):
        pl.semaphore_signal(barrier, inc=1, device_id=yp(k), device_id_type=MESH)
    for k in range(1, NZ):
        pl.semaphore_signal(barrier, inc=1, device_id=zp(k), device_id_type=MESH)
    pl.semaphore_signal(barrier, inc=1, device_id=cp, device_id_type=MESH)
    pl.semaphore_wait(barrier, NX + NY + NZ - 2)

    sgather = [send(sh, shg.at[x], gs.at[k], gr.at[k], xp(k)) for k in range(1, NX)]
    tgather = [send(th, thg.at[x], gs.at[NX + k], gr.at[NX + k], xp(k)) for k in range(1, NX)]

    labc[...] = jnp.transpose(jnp.broadcast_to(lab[pl.ds(c, 1), :].astype(F32), (128, HALF)))
    maskrow = msk[pl.ds(c, 1), :].astype(F32)
    mskc[...] = jnp.transpose(jnp.broadcast_to(maskrow, (128, HALF)))

    def scores(gathered, table, depth, sent, own):
        def rows(which):
            return gathered[pl.ds(2 * which, 2)].reshape(HALF, depth)

        for n in range(0, VB, 256):
            sent[:, n : n + 256] = nt(rows(1 - c), table[n : n + 256, :]).astype(sent.dtype)

        def rest():
            for n in range(0, VB, 256):
                own[:, n : n + 256] = nt(rows(c), table[n : n + 256, :])

        return rest

    loads[0].wait()
    loads[2].wait()
    arrive(sgather)
    rest = scores(shg, sev, DS, ssend, sown)
    score_s = send(ssend, srecv, cs.at[0], cr.at[0], cp)
    rest()

    score_s.wait_recv()
    lane = lax.broadcasted_iota(jnp.int32, (32, 128), 1)
    column = lax.broadcasted_iota(jnp.int32, (32, VB), 1) + (v * NX + x) * VB
    columnf = column.astype(F32)

    def student(i, carry):
        at = pl.ds(pl.multiple_of(i * 32, 32), 32)
        b = jnp.tanh((sown[at, :] + srecv[at, :]) / CAP)
        s = jnp.exp((CAP / 2) * b)
        bnd[at, :] = b
        soft[at, :] = s
        hit = jnp.where(columnf == labc[at, 0:1], b, 0.0)
        total = jnp.sum(s, axis=1, keepdims=True)
        hard = jnp.sum(s * s, axis=1, keepdims=True)
        label = CAP * jnp.sum(hit, axis=1, keepdims=True)
        stat[at, :] = jnp.where(lane == 1, total, jnp.where(lane == 2, hard, jnp.where(lane == 4, label, 0.0)))
        return carry

    lax.fori_loop(0, HALF // 32, student, 0)

    loads[1].wait()
    loads[3].wait()
    arrive(tgather)
    rest = scores(thg, tev, DT, tsend, town)
    score_t = send(tsend, trecv, cs.at[1], cr.at[1], cp)
    rest()
    score_t.wait_recv()

    def teacher(i, carry):
        at = pl.ds(pl.multiple_of(i * 32, 32), 32)
        t = jnp.tanh((town[at, :] + trecv[at, :].astype(F32)) / CAP)
        w = jnp.exp((CAP / 2) * t).astype(BF16)
        wts[at, :] = w
        w = w.astype(F32)
        total = jnp.sum(w, axis=1, keepdims=True)
        cross = CAP * jnp.sum(w * bnd[at, :], axis=1, keepdims=True)
        stat[at, :] = jnp.where(lane == 0, total, jnp.where(lane == 3, cross, stat[at, :]))
        return carry

    lax.fori_loop(0, HALF // 32, teacher, 0)

    def everywhere(slots, me, n, peer, value, ssem, rsem):
        slots[pl.ds(me, 1)] = value[None]
        copies = [send(slots.at[me], slots.at[me], ssem.at[k - 1], rsem.at[k - 1], peer(k)) for k in range(1, n)]
        arrive(copies)
        return jnp.sum(slots[...], axis=0), copies

    part = jnp.transpose(stat[...])[0:8, :]
    part, stat_x = everywhere(sx, x, NX, xp, part, xs, xr)
    part, stat_y = everywhere(sy, y, NY, yp, part, ys, yr)
    part, stat_z = everywhere(sz, z, NZ, zp, part, zs, zr)
    statc[...] = jnp.transpose(jnp.concatenate([part, jnp.ones((120, HALF), F32)], axis=0))

    per_token = 2.0 * (jnp.log(part[1:2]) - 0.5 * part[3:4] / part[0:1]) + 0.5 * (jnp.log(part[2:3]) - part[4:5])
    lost = jnp.sum(maskrow * per_token, axis=1, keepdims=True)
    lbuf[...] = jnp.broadcast_to(lost, (8, 128))
    loss_c = send(lbuf, lrecv, cs.at[2], cr.at[2], cp)

    def grad(i, carry):
        at = pl.ds(pl.multiple_of(i * 32, 32), 32)
        m = mskc[at, 0:1]
        b, s = bnd[at, :], soft[at, :]
        rt, rs, rh = m / statc[at, 0:1], m / statc[at, 1:2], 0.5 * m / statc[at, 2:3]
        g = s * (rs + rh * s) - wts[at, :].astype(F32) * rt
        g = g - jnp.where(columnf == labc[at, 0:1], 0.5 * m, 0.0)
        gfull[c, at, :] = (g * (1.0 - b * b)).astype(BF16)
        return carry

    lax.fori_loop(0, HALF // 32, grad, 0)
    grad_c = send(gfull.at[c], gfull.at[c], cs.at[3], cr.at[3], cp)
    grad_c.wait_recv()

    def product(first, width):
        out = []
        for h in range(2):
            out.append(jnp.dot(gfull[h], sev[:, first : first + width], preferred_element_type=F32).astype(BF16))
        return out

    def fill(dst, first, width, at):
        for h, block in enumerate(product(first, width)):
            dst[2 * h : 2 * h + 2, :, :, at : at + width] = block.reshape(2, 8, 16, width)

    for n in range(0, CXY, 256):
        fill(gx, n, 256, n)
        fill(gx, CA + n, 256, CXY + n)
    out_x = [send(gx.at[xi(k)], rx.at[k - 1], x1s.at[k - 1], x1r.at[k - 1], xp(k)) for k in range(1, NX)]
    fill(gy, CXY, CYX, 0)
    out_y = [send(gy.at[:, yi(k)], ry.at[k - 1], y1s.at[k - 1], y1r.at[k - 1], yp(k)) for k in range(1, NY)]
    fill(gz, CA + CXY, CYX, 0)
    out_z = [send(gz.at[:, zi(k)], rz.at[k - 1], z1s.at[k - 1], z1r.at[k - 1], zp(k)) for k in range(1, NZ)]

    arrive(out_x)
    for j in range(8):
        total = gx[x, j].astype(F32)
        for k in range(NX - 1):
            total = total + rx[k, j].astype(F32)
        total = total.astype(BF16)
        hxy[j] = total[:, :CXY]
        hxz[j] = total[:, CXY:]
    out_xy = [send(hxy.at[yi(k)], r2y.at[k - 1], y2s.at[k - 1], y2r.at[k - 1], yp(k)) for k in range(1, NY)]
    out_xz = [send(hxz.at[zi(k)], r2z.at[k - 1], z2s.at[k - 1], z2r.at[k - 1], zp(k)) for k in range(1, NZ)]
    arrive(out_y)
    for q in range(NX):
        total = gy[q, y].astype(F32)
        for k in range(NY - 1):
            total = total + ry[k, q].astype(F32)
        hx2[q, 0] = total.astype(BF16)
    arrive(out_z)
    for q in range(NX):
        total = gz[q, z].astype(F32)
        for k in range(NZ - 1):
            total = total + rz[k, q].astype(F32)
        hx2[q, 1] = total.astype(BF16)
    out_yx = [send(hx2.at[xi(k)], r2x.at[k - 1], x2s.at[k - 1], x2r.at[k - 1], xp(k)) for k in range(1, NX)]

    arrive(out_xy)
    total = hxy[y].astype(F32)
    for k in range(NY - 1):
        total = total + r2y[k].astype(F32)
    ra[z, :, 0:CXY] = total.astype(BF16)
    arrive(out_xz)
    total = hxz[z].astype(F32)
    for k in range(NZ - 1):
        total = total + r2z[k].astype(F32)
    rb[y, :, 0:CXY] = total.astype(BF16)
    arrive(out_yx)
    for i, dst, me in ((0, ra, z), (1, rb, y)):
        total = hx2[x, i].astype(F32)
        for k in range(NX - 1):
            total = total + r2x[k, i].astype(F32)
        dst[me, :, CXY:CA] = total.astype(BF16)
    all_a = [send(ra.at[z], ra.at[z], az.at[k - 1], azr.at[k - 1], zp(k)) for k in range(1, NZ)]
    all_b = [send(rb.at[y], rb.at[y], by.at[k - 1], byr.at[k - 1], yp(k)) for k in range(1, NY)]
    arrive(all_a)
    outv[y, :, 0:CA] = jnp.sum(ra[...].astype(F32), axis=0).astype(BF16)
    spread_a = [
        send(outv.at[y, :, pl.ds(0, CA)], outv.at[y, :, pl.ds(0, CA)], ay.at[k - 1], ayr.at[k - 1], yp(k))
        for k in range(1, NY)
    ]
    arrive(all_b)
    outv[z, :, CA:DS] = jnp.sum(rb[...].astype(F32), axis=0).astype(BF16)
    spread_b = [
        send(outv.at[z, :, pl.ds(CA, CA)], outv.at[z, :, pl.ds(CA, CA)], bz.at[k - 1], bzr.at[k - 1], zp(k))
        for k in range(1, NZ)
    ]
    loss_c.wait_recv()
    count = jnp.sum(msk[...].astype(F32), keepdims=True)
    loss_ref[...] = (lbuf[0:1, 0:1] + lrecv[0:1, 0:1]) / jnp.maximum(count, 1.0)
    for group in (
        sgather, tgather, [score_s, score_t, loss_c, grad_c], stat_x, stat_y, stat_z,
        out_x, out_y, out_z, out_xy, out_xz, out_yx, all_a, all_b,
    ):
        leave(group)
    arrive(spread_a)
    arrive(spread_b)
    leave(spread_a)
    leave(spread_b)
    done = pltpu.make_async_copy(outv, out_ref, lsem.at[4])
    done.start()
    done.wait()


def shards(th, te, sh, se, labels, mask):
    hbm = pl.BlockSpec(memory_space=pl.ANY)
    vmem = pl.BlockSpec(memory_space=pltpu.VMEM)
    V = pltpu.VMEM

    def sems(n):
        return pltpu.SemaphoreType.DMA((n,))

    loss, grad = pl.pallas_call(
        body,
        out_shape=(jax.ShapeDtypeStruct((1, 1), F32), jax.ShapeDtypeStruct((8, 16, DS), BF16)),
        in_specs=[hbm, hbm, hbm, hbm, vmem, vmem],
        out_specs=(vmem, hbm),
        scratch_shapes=[
            V((NX, QUARTER, DT), BF16), V((NX, QUARTER, DS), BF16), V((VB, DT), BF16), V((VB, DS), BF16),
            V((HALF, VB), BF16), V((HALF, VB), BF16), V((HALF, VB), F32),
            V((HALF, VB), F32), V((HALF, VB), F32), V((HALF, VB), F32),
            V((HALF, VB), BF16), V((HALF, VB), F32), V((HALF, VB), F32),
            V((HALF, 128), F32), V((HALF, 128), F32), V((HALF, 128), F32), V((HALF, 128), F32),
            V((NX, 8, HALF), F32), V((NY, 8, HALF), F32), V((NZ, 8, HALF), F32),
            V((8, 128), F32), V((8, 128), F32),
            V((2, HALF, VB), BF16),
            V((NX, 8, 16, 2 * CXY), BF16), V((NX, 8, 16, CYX), BF16), V((NX, 8, 16, CYX), BF16),
            V((NX - 1, 8, 16, 2 * CXY), BF16), V((NY - 1, NX, 16, CYX), BF16), V((NZ - 1, NX, 16, CYX), BF16),
            V((8, 16, CXY), BF16), V((8, 16, CXY), BF16), V((NY - 1, 16, CXY), BF16), V((NZ - 1, 16, CXY), BF16),
            V((NX, 2, 16, CYX), BF16), V((NX - 1, 2, 16, CYX), BF16),
            V((16, CA), BF16), V((16, CA), BF16), V((NZ, 16, CA), BF16), V((NY, 16, CA), BF16),
            V((8, 16, DS), BF16),
            sems(5), sems(8), sems(8), sems(4), sems(4),
            sems(3), sems(3), sems(7), sems(7), sems(7), sems(7),
            sems(3), sems(3), sems(7), sems(7), sems(7), sems(7),
            sems(3), sems(3), sems(7), sems(7), sems(7), sems(7),
            sems(7), sems(7), sems(7), sems(7), sems(7), sems(7), sems(7), sems(7),
        ],
        compiler_params=pltpu.CompilerParams(
            collective_id=0, has_side_effects=True, vmem_limit_bytes=56 * 2**20
        ),
        name="distill",
    )(th, te, sh, se, labels.reshape(2, HALF), mask.reshape(2, HALF))
    return loss.reshape(()), grad.reshape(QUARTER, DS)


def solution(mesh):
    placed = (
        P("rep", "inner"),
        P(("vocab", "rep"), "inner"),
        P("rep", "inner"),
        P(("vocab", "rep"), "inner"),
        P(),
        P(),
    )
    return jax.shard_map(
        shards, mesh=mesh, in_specs=placed, out_specs=(P(), P("rep", "inner")), check_vma=False
    )
```

time: 2240 us -> 129 us (0.06)
  blocking collectives: 2090 us -> 0 us
  Pallas kernels: 0 us -> 122 us
  waiting for transfers between devices: 114 us -> 0 us
    psum x3 -> x0, blocking collectives: 1980 us -> none  [the longest x2 1760 us: shards(): lax.psum((jnp.sum(teacher_exp_values, axis=1), soft_part, hard_part, cros...]
    pallas_call x0 -> x1, Pallas kernels: none -> 122 us  [shards(): pl.pallas_call(body, out_shape=(jax.ShapeDtypeStruct((1, 1), F32), jax.Sh...]
    all_gather x1 -> x0, blocking collectives: 113 us -> none  [shards(): grad_all = lax.all_gather(logit_grad, 'inner', axis=0, tiled=True)]
    all_gather x2 -> x0, waiting for transfers between devices: 77.5 us -> none  [the longest x1 45.3 us: shards(): lax.all_gather(teacher_hidden, 'rep', axis=0, tiled=True)]
    reduce_scatter x2 -> x0, waiting for transfers between devices: 35.2 us -> none  [the longest x1 19.8 us: shards(): lax.psum_scatter(student_part, 'inner', scatter_dimension=0, tiled=True)]
  transfers between devices with their start and end apart: 4 -> 0, of which waited for: 4 -> 0; matrix products, arithmetic and copies ran while one was open for 0% -> 0% of each run, Pallas kernels for 0% -> 0%
where the time goes in v1:
time: 129 us
  Pallas kernels  122 us (95%)
  local copies, waits for them, and re-layouts  4.37 us (3%)
  between operations  2.4 us (2%)
    pallas_call x1, Pallas kernels, shards(): pl.pallas_call(body, out_shape=(jax.ShapeDtypeStruct((1, 1), F32), jax.Sh...  122 us

profile of v1, /device:TPU:1, one launch (start us, length us, event | category | flops | bytes accessed | tf_op | source)
XLA Modules:
  0.0 128.7 jit_solution(16799175241573502846)
XLA Ops:
  0.6 1.3 reshape.16.lab
  1.9 1.3 reshape.17.msk
  3.2 122.0 %distill.1 = (f32[1,1]{1,0:T(1,128)}, bf16[8,16,1792]{2,1,0:T(8,128)(2,1)}) custom-call(bf16[128,2304]{1,0:T(8,128)(2,1)} %th.1, bf16[512,2304]{1,0:T(8,128)(2,1)} %te.1, bf16[128,1792]{1,0:T(8,128)(2,1)} %sh.1, bf16[512,1792]{1,0:T(8,128)(2,1)} %se.1, s32[2,256]{1,0:T(2,128)} %reshape.16.lab, s32[2,256]{1,0:T(2,128)} %reshape.17.msk), custom_call_target="tpu_custom_call" | custom-call | tf_op jit(solution)/shard_map/distill/pallas_call | solution.py:288
  125.8 1.8 %copy.11 = bf16[128,1792]{1,0:T(8,128)(2,1)} copy(bf16[128,1792]{1,0:T(8,128)(2,1)} %bitcast.2) | data formatting | bytes 917504

commit v2 on v1

v2 whole, which is shorter than its diff:
```python
import jax
import jax.numpy as jnp
from jax import lax
from jax.experimental import pallas as pl
from jax.experimental.pallas import tpu as pltpu
from jax.sharding import PartitionSpec as P

MESH = pl.DeviceIdType.MESH
CAP = 30.0
NX, NY, NZ = 4, 8, 8
TOK, DT, DS, VB = 512, 2304, 1792, 512
HALF = TOK // 2
QUARTER = TOK // NX
CX = 256
CHUNKS = ((0, 512, 384), (896, 384, 512))
F32, BF16 = jnp.float32, jnp.bfloat16
STUDENT_PARTS = ((0, 512, "y", 0, 0), (512, 512, "z", 0, 1), (1024, 384, "y", 1, 1), (1408, 384, "z", 1, 0))
TEACHER_PARTS = ((0, 640, "y", 0, 1), (640, 640, "z", 0, 0), (1280, 512, "y", 1, 0), (1792, 512, "z", 1, 1))
FAR_FIRST = (4, 3, 5, 2, 6, 1, 7)


class Fixed:
    def __init__(self, ref, index):
        self.ref, self.index = ref, index

    @property
    def at(self):
        return self

    def __getitem__(self, _):
        return self.ref.at[self.index]


class Same(Fixed):
    def __init__(self, ref):
        self.ref = ref

    def __getitem__(self, _):
        return self.ref


def nt(left, right):
    return lax.dot_general(left, right, (((1,), (1,)), ((), ())), preferred_element_type=F32)


def body(
    th, te, sh, se, lab, msk, loss_ref, out_ref,
    thg, shg, tev, sev,
    tsend, trecv, town, ssend, srecv, sown,
    wts, soft, bnd, labc, mskc, stat, statc, sx, sy, sz, ux, uy, uz, lbuf, lrecv,
    gfull, outv,
    lsem, gs, gr, cs, cr, xs, xr, ys, yr, zs, zr, uxs, uxr, uys, uyr, uzs, uzr, x1s, x1r, y1s, y1r, z1s, z1r,
    x2s, x2r, x3s, x3r, y2s, y2r, z2s, z2r, azs, azr, bys, byr, ays, ayr, bzs, bzr, *rest_bufs,
):
    bufs = [rest_bufs[16 * i : 16 * i + 16] for i in range(len(CHUNKS))]
    v = lax.axis_index("vocab")
    c = lax.axis_index("inner")
    x = lax.axis_index("rep")
    z, y = v // NY, v % NY

    def xi(k):
        return lax.rem(x + k, NX)

    def yi(k):
        return lax.rem(y + k, NY)

    def zi(k):
        return lax.rem(z + k, NZ)

    def xp(k):
        return (v, c, xi(k))

    def yp(k):
        return (z * NY + yi(k), c, x)

    def zp(k):
        return (zi(k) * NY + y, c, x)

    cp = (v, 1 - c, x)
    flip = (x, x + 1 - 2 * (x % 2), x + 2 - 4 * (x // 2), 3 - x)
    odd = x % 2

    def send(src, dst, ssem, rsem, to):
        copy = pltpu.make_async_remote_copy(
            src_ref=src, dst_ref=dst, send_sem=ssem, recv_sem=rsem, device_id=to, device_id_type=MESH
        )
        copy.start()
        return copy

    def arrive(copies):
        for copy in copies:
            copy.wait_recv()

    def leave(copies):
        for copy in copies:
            copy.wait_send()

    loads = [
        pltpu.make_async_copy(se, sev, lsem.at[0]),
        pltpu.make_async_copy(te, tev, lsem.at[1]),
        pltpu.make_async_copy(sh, shg.at[0], lsem.at[2]),
        pltpu.make_async_copy(th, thg.at[0], lsem.at[3]),
    ]
    for load in loads:
        load.start()

    barrier = pltpu.get_barrier_semaphore()
    others = [xp(k) for k in (2, 1, 3)] + [cp]
    others = [p(k) for k in FAR_FIRST for p in (yp, zp)] + others
    for other in others:
        pl.semaphore_signal(barrier, inc=1, device_id=other, device_id_type=MESH)
    pl.semaphore_wait(barrier, len(others))

    def gather(source, buffer, parts, base):
        out = []
        for p, (first, width, order, shift_y, shift_z) in enumerate(parts):
            cols = pl.ds(first, width)
            bit_y, bit_z = (y + shift_y) % 2, (z + shift_z) % 2
            pair_y, pair_z = yp(NY + 1 - 2 * bit_y), zp(NZ + 1 - 2 * bit_z)
            if order == "y":
                bf, bs, pf, ps = bit_y, bit_z, pair_y, pair_z
            else:
                bf, bs, pf, ps = bit_z, bit_y, pair_z, pair_y
            i = base + p
            copies = [
                send(source.at[:, bs, bf, :, cols], buffer.at[k, :, bs, bf, :, cols],
                     gs.at[i, k], gr.at[i, k], (v, c, flip[k]))
                for k in (2, 1, 3)
            ]

            def first_swap(copies=copies, i=i, bs=bs, bf=bf, cols=cols, pf=pf):
                arrive(copies)
                block = buffer.at[pl.ds(1, 3), :, bs, bf, :, cols]
                return send(block, block, gs.at[i, 0], gr.at[i, 0], pf)

            def second_swap(swapped, i=i, bs=bs, cols=cols, ps=ps):
                arrive([swapped])
                block = buffer.at[pl.ds(1, 3), :, bs, :, :, cols]
                return send(block, block, gs.at[i, 4], gr.at[i, 4], ps)

            gathers.extend(copies)
            out.append((first_swap, second_swap))
        return out

    gathers = []
    parts = gather(sh, shg, STUDENT_PARTS, 0) + gather(th, thg, TEACHER_PARTS, 4)

    def row(ref):
        whole = ref[...].astype(F32).reshape(1, TOK)
        return jnp.where(c == 0, whole[:, :HALF], whole[:, HALF:])

    labc[...] = jnp.transpose(jnp.broadcast_to(row(lab), (128, HALF)))
    maskrow = row(msk)
    mskc[...] = jnp.transpose(jnp.broadcast_to(maskrow, (128, HALF)))

    once, twice = [], []
    for p in range(4):
        once.append(parts[p][0]())
    for p in range(4):
        twice.append(parts[p][1](once[p]))
        once.append(parts[4 + p][0]())
    for p in range(4, 8):
        twice.append(parts[p][1](once[p]))

    def scores(gathered, table, depth, sent, own):
        def block(which, n, into):
            pair = which + x // 2 - 2 * which * (x // 2)
            rows = gathered[pl.ds(2 * pair, 2)].reshape(HALF, depth)
            out = nt(rows, table[n : n + 256, :]).astype(into.dtype)
            into[odd, :, n : n + 256] = out[:QUARTER]
            into[1 - odd, :, n : n + 256] = out[QUARTER:]

        for n in range(0, VB, 256):
            block(1 - c, n, sent)

        def rest():
            for n in range(0, VB, 256):
                block(c, n, own)

        return rest

    loads[0].wait()
    loads[2].wait()
    arrive(twice[:4])
    rest = scores(shg, sev, DS, ssend, sown)
    score_s = send(ssend, srecv, cs.at[0], cr.at[0], cp)
    rest()

    score_s.wait_recv()
    lane = lax.broadcasted_iota(jnp.int32, (32, 128), 1)
    column = lax.broadcasted_iota(jnp.int32, (32, VB), 1) + (v * NX + x) * VB
    columnf = column.astype(F32)

    def student(i, carry):
        at = pl.ds(pl.multiple_of(i * 32, 32), 32)
        h, w = i // 4, pl.ds(pl.multiple_of((i % 4) * 32, 32), 32)
        b = jnp.tanh((sown[h, w, :] + srecv[h, w, :]) / CAP)
        s = jnp.exp((CAP / 2) * b)
        bnd[at, :] = b
        soft[at, :] = s
        hit = jnp.where(columnf == labc[at, 0:1], b, 0.0)
        total = jnp.sum(s, axis=1, keepdims=True)
        hard = jnp.sum(s * s, axis=1, keepdims=True)
        label = CAP * jnp.sum(hit, axis=1, keepdims=True)
        stat[at, :] = jnp.where(lane == 1, total, jnp.where(lane == 2, hard, jnp.where(lane == 4, label, 0.0)))
        return carry

    lax.fori_loop(0, HALF // 32, student, 0)

    loads[1].wait()
    loads[3].wait()
    arrive(twice[4:])
    rest = scores(thg, tev, DT, tsend, town)
    score_t = send(tsend, trecv, cs.at[1], cr.at[1], cp)
    rest()
    score_t.wait_recv()

    def teacher(i, carry):
        at = pl.ds(pl.multiple_of(i * 32, 32), 32)
        h, w = i // 4, pl.ds(pl.multiple_of((i % 4) * 32, 32), 32)
        t = jnp.tanh((town[h, w, :] + trecv[h, w, :].astype(F32)) / CAP)
        e = jnp.exp((CAP / 2) * t).astype(BF16)
        wts[at, :] = e
        e = e.astype(F32)
        total = jnp.sum(e, axis=1, keepdims=True)
        cross = CAP * jnp.sum(e * bnd[at, :], axis=1, keepdims=True)
        stat[at, :] = jnp.where(lane == 0, total, jnp.where(lane == 3, cross, stat[at, :]))
        return carry

    lax.fori_loop(0, HALF // 32, teacher, 0)

    def spread(slots, me, order, peer, value, ssem, rsem):
        slots[pl.ds(me, 1)] = value[None]
        return [send(slots.at[me], slots.at[me], ssem.at[k - 1], rsem.at[k - 1], peer(k)) for k in order]

    def collect(slots, copies):
        arrive(copies)
        stats.extend(copies)
        return jnp.sum(slots[...], axis=0)

    stats = []
    low, high = jnp.transpose(stat[0:QUARTER, :]), jnp.transpose(stat[QUARTER:HALF, :])

    def tile(*rows):
        both = [piece[r : r + 1] for r in rows for piece in (low, high)]
        return jnp.concatenate(both + [jnp.zeros((8 - len(both), 128), F32)], axis=0)

    sent = spread(sx, x, (2, 1, 3), xp, tile(0, 1, 2), xs, xr)
    aux = spread(ux, x, (2, 1, 3), xp, tile(3, 4), uxs, uxr)
    part = collect(sx, sent)
    part = collect(sy, spread(sy, y, FAR_FIRST, yp, part, ys, yr))
    part = collect(sz, spread(sz, z, FAR_FIRST, zp, part, zs, zr))
    statc[...] = jnp.transpose(jnp.concatenate([part, jnp.ones((120, 128), F32)], axis=0))

    for h in range(2):
        def grad(i, carry, h=h):
            at = pl.ds(pl.multiple_of(h * QUARTER + i * 32, 32), 32)
            w = pl.ds(pl.multiple_of(i * 32, 32), 32)
            m = mskc[at, 0:1]
            b, s = bnd[at, :], soft[at, :]
            rt, rs = m / statc[w, h : h + 1], m / statc[w, 2 + h : 3 + h]
            rh = 0.5 * m / statc[w, 4 + h : 5 + h]
            g = s * (rs + rh * s) - wts[at, :].astype(F32) * rt
            g = g - jnp.where(columnf == labc[at, 0:1], 0.5 * m, 0.0)
            gfull[c, at, :] = (g * (1.0 - b * b)).astype(BF16)
            return carry

        lax.fori_loop(0, QUARTER // 32, grad, 0)
    grad_c = send(gfull.at[c], gfull.at[c], cs.at[3], cr.at[3], cp)
    aux = spread(uy, y, FAR_FIRST, yp, collect(ux, aux), uys, uyr)

    def reduction(index, first, wide_a, wide_b):
        gx, gy, gz, rx, ry, rz, hxy, hxz, r2y, r2z, hy, hz, ry2, rz2, ra, rb = bufs[index]
        n = index
        rest_a, rest_b = wide_a - CX, wide_b - CX
        mid, last = first + wide_a, first + wide_a + wide_b

        def fill(which):
            def one(dst, at, start, width):
                block = jnp.dot(gfull[which], sev[:, start : start + width], preferred_element_type=F32)
                dst[pl.ds(2 * which, 2), :, :, at : at + width] = block.astype(BF16).reshape(2, 8, 16, width)

            one(gx, 0, first, CX)
            one(gx, CX, mid, CX)
            one(gy, 0, first + CX, rest_a)
            one(gz, 0, mid + CX, rest_b)

        def over(src, dst, order, peer, index_of, ssem, rsem):
            return [
                send(src(index_of(k)), dst.at[k - 1], ssem.at[n, k - 1], rsem.at[n, k - 1], peer(k)) for k in order
            ]

        def total(mine, received):
            out = mine.astype(F32)
            for block in received:
                out = out + block.astype(F32)
            return out.astype(BF16)

        def stage1():
            out_x = over(lambda q: gx.at[q], rx, (2, 1, 3), xp, xi, x1s, x1r)
            out_y = over(lambda j: gy.at[:, j], ry, FAR_FIRST, yp, yi, y1s, y1r)
            out_z = over(lambda j: gz.at[:, j], rz, FAR_FIRST, zp, zi, z1s, z1r)
            done.extend(out_x + out_y + out_z)
            return out_x, out_y, out_z

        def stage2(sent):
            arrive(sent[1])
            for q in range(NX):
                hy[q] = total(gy[q, y], [ry[k, q] for k in range(NY - 1)])
            out_yx = over(lambda q: hy.at[q], ry2, (2, 1, 3), xp, xi, x2s, x2r)
            arrive(sent[2])
            for q in range(NX):
                hz[q] = total(gz[q, z], [rz[k, q] for k in range(NZ - 1)])
            out_zx = over(lambda q: hz.at[q], rz2, (2, 1, 3), xp, xi, x3s, x3r)
            arrive(sent[0])
            for j in range(8):
                both = total(gx[x, j], [rx[k, j] for k in range(NX - 1)])
                hxy[j] = both[:, :CX]
                hxz[j] = both[:, CX:]
            out_xy = over(lambda j: hxy.at[j], r2y, FAR_FIRST, yp, yi, y2s, y2r)
            out_xz = over(lambda j: hxz.at[j], r2z, FAR_FIRST, zp, zi, z2s, z2r)
            done.extend(out_yx + out_zx + out_xy + out_xz)
            return out_yx, out_zx, out_xy, out_xz

        def stage3(sent):
            arrive(sent[0])
            ra[z, :, CX:wide_a] = total(hy[x], [ry2[k] for k in range(NX - 1)])
            arrive(sent[1])
            rb[y, :, CX:wide_b] = total(hz[x], [rz2[k] for k in range(NX - 1)])
            arrive(sent[2])
            ra[z, :, 0:CX] = total(hxy[y], [r2y[k] for k in range(NY - 1)])
            all_a = over(lambda _: ra.at[z], Fixed(ra, z), FAR_FIRST, zp, zi, azs, azr)
            arrive(sent[3])
            rb[y, :, 0:CX] = total(hxz[z], [r2z[k] for k in range(NZ - 1)])
            all_b = over(lambda _: rb.at[y], Fixed(rb, y), FAR_FIRST, yp, yi, bys, byr)
            done.extend(all_a + all_b)
            return all_a, all_b

        def stage4(sent):
            cols_a, cols_b = pl.ds(first, wide_a), pl.ds(mid, wide_b)
            arrive(sent[0])
            outv[y, :, cols_a] = jnp.sum(ra[...].astype(F32), axis=0).astype(BF16)
            here = outv.at[y, :, cols_a]
            out_a = over(lambda _: here, Same(here), FAR_FIRST, yp, yi, ays, ayr)
            arrive(sent[1])
            outv[z, :, cols_b] = jnp.sum(rb[...].astype(F32), axis=0).astype(BF16)
            there = outv.at[z, :, cols_b]
            out_b = over(lambda _: there, Same(there), FAR_FIRST, zp, zi, bzs, bzr)
            return out_a + out_b

        return fill, stage1, stage2, stage3, stage4

    done = []
    chunks = [reduction(i, *chunk) for i, chunk in enumerate(CHUNKS)]
    for fill, *_ in chunks[:1]:
        fill(c)
    grad_c.wait_recv()
    pipe = []
    for i, chunk in enumerate(chunks):
        if i > 0:
            chunk[0](c)
        chunk[0](1 - c)
        pipe.append(chunk[1]())
    aux = spread(uz, z, FAR_FIRST, zp, collect(uy, aux), uzs, uzr)
    pipe = [chunk[2](sent) for chunk, sent in zip(chunks, pipe)]
    rest_of = collect(uz, aux)
    lost = jnp.zeros((1, 1), F32)
    for h in range(2):
        per_token = 2.0 * (jnp.log(part[2 + h : 3 + h]) - 0.5 * rest_of[h : h + 1] / part[h : h + 1])
        per_token = per_token + 0.5 * (jnp.log(part[4 + h : 5 + h]) - rest_of[2 + h : 3 + h])
        owned = maskrow[:, h * QUARTER : (h + 1) * QUARTER]
        lost = lost + jnp.sum(owned * per_token, axis=1, keepdims=True)
    lbuf[...] = jnp.broadcast_to(lost, (8, 128))
    loss_c = send(lbuf, lrecv, cs.at[2], cr.at[2], cp)
    pipe = [chunk[3](sent) for chunk, sent in zip(chunks, pipe)]
    pipe = [chunk[4](sent) for chunk, sent in zip(chunks, pipe)]
    loss_c.wait_recv()
    count = jnp.sum(msk[...].astype(F32).reshape(1, TOK), axis=1, keepdims=True)
    loss_ref[...] = (lbuf[0:1, 0:1] + lrecv[0:1, 0:1]) / jnp.maximum(count, 1.0)
    for group in (gathers, once, twice, [score_s, score_t, loss_c, grad_c], stats, done):
        leave(group)
    for copies in pipe:
        arrive(copies)
    for copies in pipe:
        leave(copies)
    result = pltpu.make_async_copy(outv, out_ref, lsem.at[4])
    result.start()
    result.wait()


def shards(th, te, sh, se, labels, mask):
    hbm = pl.BlockSpec(memory_space=pl.ANY)
    vmem = pl.BlockSpec(memory_space=pltpu.VMEM)
    V = pltpu.VMEM

    def sems(n):
        return pltpu.SemaphoreType.DMA((n,))

    def each(n):
        return pltpu.SemaphoreType.DMA((len(CHUNKS), n))

    loss, grad = pl.pallas_call(
        body,
        out_shape=(jax.ShapeDtypeStruct((1, 1), F32), jax.ShapeDtypeStruct((8, 16, DS), BF16)),
        in_specs=[hbm, hbm, hbm, hbm, vmem, vmem],
        out_specs=(vmem, hbm),
        scratch_shapes=[
            V((NX, 2, 2, 2, 16, DT), BF16), V((NX, 2, 2, 2, 16, DS), BF16), V((VB, DT), BF16), V((VB, DS), BF16),
            V((2, QUARTER, VB), BF16), V((2, QUARTER, VB), BF16), V((2, QUARTER, VB), F32),
            V((2, QUARTER, VB), F32), V((2, QUARTER, VB), F32), V((2, QUARTER, VB), F32),
            V((HALF, VB), BF16), V((HALF, VB), F32), V((HALF, VB), F32),
            V((HALF, 128), F32), V((HALF, 128), F32), V((HALF, 128), F32), V((QUARTER, 128), F32),
            V((NX, 8, 128), F32), V((NY, 8, 128), F32), V((NZ, 8, 128), F32),
            V((NX, 8, 128), F32), V((NY, 8, 128), F32), V((NZ, 8, 128), F32),
            V((8, 128), F32), V((8, 128), F32),
            V((2, HALF, VB), BF16),
            V((8, 16, DS), BF16),
            sems(5), pltpu.SemaphoreType.DMA((8, 5)), pltpu.SemaphoreType.DMA((8, 5)), sems(4), sems(4),
            sems(3), sems(3), sems(7), sems(7), sems(7), sems(7),
            sems(3), sems(3), sems(7), sems(7), sems(7), sems(7),
            each(3), each(3), each(7), each(7), each(7), each(7),
            each(3), each(3), each(3), each(3), each(7), each(7), each(7), each(7),
            each(7), each(7), each(7), each(7), each(7), each(7), each(7), each(7),
            *[
                V(shape, BF16)
                for _, wide_a, wide_b in CHUNKS
                for ca, cb in ((wide_a - CX, wide_b - CX),)
                for shape in (
                    (NX, 8, 16, 2 * CX), (NX, 8, 16, ca), (NX, 8, 16, cb),
                    (NX - 1, 8, 16, 2 * CX), (NY - 1, NX, 16, ca), (NZ - 1, NX, 16, cb),
                    (8, 16, CX), (8, 16, CX), (NY - 1, 16, CX), (NZ - 1, 16, CX),
                    (NX, 16, ca), (NX, 16, cb), (NX - 1, 16, ca), (NX - 1, 16, cb),
                    (NZ, 16, wide_a), (NY, 16, wide_b),
                )
            ],
        ],
        compiler_params=pltpu.CompilerParams(
            collective_id=0, has_side_effects=True, vmem_limit_bytes=56 * 2**20
        ),
        name="distill",
    )(th.reshape(2, 2, 2, 16, DT), te, sh.reshape(2, 2, 2, 16, DS), se, labels, mask)
    return loss.reshape(()), grad.reshape(QUARTER, DS)


def solution(mesh):
    placed = (
        P("rep", "inner"),
        P(("vocab", "rep"), "inner"),
        P("rep", "inner"),
        P(("vocab", "rep"), "inner"),
        P(),
        P(),
    )
    return jax.shard_map(
        shards, mesh=mesh, in_specs=placed, out_specs=(P(), P("rep", "inner")), check_vma=False
    )
```

time: 129 us -> 98.1 us (0.76)
  Pallas kernels: 122 us -> 93.6 us
  local copies, waits for them, and re-layouts: 4.37 us -> 1.82 us
    pallas_call x1, Pallas kernels: 122 us -> 93.6 us  [shards(): pl.pallas_call(body, out_shape=(jax.ShapeDtypeStruct((1, 1), F32), jax.Sh...]
    reshape x2 -> x0, local copies, waits for them, and re-layouts: 2.55 us -> none  [the longest x1 1.28 us: shards(): mask.reshape(2, HALF)]
where the time goes in v2:
time: 98.1 us; the launch traced here: 97.8 us
  Pallas kernels  93.6 us (95%)
  between operations  2.45 us (2%)
  local copies, waits for them, and re-layouts  1.82 us (2%)
    pallas_call x1, Pallas kernels, shards(): pl.pallas_call(body, out_shape=(jax.ShapeDtypeStruct((1, 1), F32), jax.Sh...  93.6 us

profile of v2, /device:TPU:1, one launch (start us, length us, event | category | flops | bytes accessed | tf_op | source)
XLA Modules:
  0.0 97.8 jit_solution(10381147655618096485)
XLA Ops:
  0.6 93.6 %distill.1 = (f32[1,1]{1,0:T(1,128)}, bf16[8,16,1792]{2,1,0:T(8,128)(2,1)}) custom-call(bf16[2,2,2,16,2304]{4,3,2,1,0:T(8,128)(2,1)} %bitcast.4, bf16[512,2304]{1,0:T(8,128)(2,1)} %te.1, bf16[2,2,2,16,1792]{4,3,2,1,0:T(8,128)(2,1)} %bitcast.5, bf16[512,1792]{1,0:T(8,128)(2,1)} %se.1, s32[512]{0:T(512)} %lab.1, s32[512]{0:T(512)} %msk.1), custom_call_target="tpu_custom_call" | custom-call | tf_op jit(solution)/shard_map/distill/pallas_call | solution.py:402
  94.9 1.8 %copy.11 = bf16[128,1792]{1,0:T(8,128)(2,1)} copy(bf16[128,1792]{1,0:T(8,128)(2,1)} %bitcast.6) | data formatting | bytes 917504

commit v3 on v2

--- a/solution.py
+++ b/solution.py
@@ -15,7 +15,8 @@
 CHUNKS = ((0, 512, 384), (896, 384, 512))
 F32, BF16 = jnp.float32, jnp.bfloat16
 STUDENT_PARTS = ((0, 512, "y", 0, 0), (512, 512, "z", 0, 1), (1024, 384, "y", 1, 1), (1408, 384, "z", 1, 0))
-TEACHER_PARTS = ((0, 640, "y", 0, 1), (640, 640, "z", 0, 0), (1280, 512, "y", 1, 0), (1792, 512, "z", 1, 1))
+TEACHER_PARTS = ((0, 384, "y", 0, 1), (384, 384, "z", 0, 0), (768, 384, "y", 1, 0), (1152, 384, "z", 1, 1))
+TEACHER_REST = (1536, 768)
 FAR_FIRST = (4, 3, 5, 2, 6, 1, 7)
 
 
@@ -159,6 +160,12 @@
     for p in range(4):
         twice.append(parts[p][1](once[p]))
         once.append(parts[4 + p][0]())
+    cols = pl.ds(*TEACHER_REST)
+    alone = [
+        send(th.at[w, :, :, :, cols], thg.at[k, w, :, :, :, cols], gs.at[8 + w, k], gr.at[8 + w, k], (v, c, flip[k]))
+        for w in range(2)
+        for k in (2, 1, 3)
+    ]
     for p in range(4, 8):
         twice.append(parts[p][1](once[p]))
 
@@ -210,6 +217,7 @@
     loads[1].wait()
     loads[3].wait()
     arrive(twice[4:])
+    arrive(alone)
     rest = scores(thg, tev, DT, tsend, town)
     score_t = send(tsend, trecv, cs.at[1], cr.at[1], cp)
     rest()
@@ -377,7 +385,7 @@
     loss_c.wait_recv()
     count = jnp.sum(msk[...].astype(F32).reshape(1, TOK), axis=1, keepdims=True)
     loss_ref[...] = (lbuf[0:1, 0:1] + lrecv[0:1, 0:1]) / jnp.maximum(count, 1.0)
-    for group in (gathers, once, twice, [score_s, score_t, loss_c, grad_c], stats, done):
+    for group in (gathers, alone, once, twice, [score_s, score_t, loss_c, grad_c], stats, done):
         leave(group)
     for copies in pipe:
         arrive(copies)
@@ -415,7 +423,7 @@
             V((8, 128), F32), V((8, 128), F32),
             V((2, HALF, VB), BF16),
             V((8, 16, DS), BF16),
-            sems(5), pltpu.SemaphoreType.DMA((8, 5)), pltpu.SemaphoreType.DMA((8, 5)), sems(4), sems(4),
+            sems(5), pltpu.SemaphoreType.DMA((10, 5)), pltpu.SemaphoreType.DMA((10, 5)), sems(4), sems(4),
             sems(3), sems(3), sems(7), sems(7), sems(7), sems(7),
             sems(3), sems(3), sems(7), sems(7), sems(7), sems(7),
             each(3), each(3), each(7), each(7), each(7), each(7),

time: 98.1 us -> 95.6 us (0.975)
  Pallas kernels: 93.6 us -> 91.2 us
    pallas_call x1, Pallas kernels: 93.6 us -> 91.2 us  [shards(): pl.pallas_call(body, out_shape=(jax.ShapeDtypeStruct((1, 1), F32), jax.Sh...]
where the time goes in v3:
time: 95.6 us; the launch traced here: 95.4 us
  Pallas kernels  91.2 us (95%)
  between operations  2.45 us (3%)
  local copies, waits for them, and re-layouts  1.82 us (2%)
    pallas_call x1, Pallas kernels, shards(): pl.pallas_call(body, out_shape=(jax.ShapeDtypeStruct((1, 1), F32), jax.Sh...  91.2 us

profile of v3, /device:TPU:1, one launch (start us, length us, event | category | flops | bytes accessed | tf_op | source)
XLA Modules:
  0.0 95.4 jit_solution(11939576623525795102)
XLA Ops:
  0.6 91.2 %distill.1 = (f32[1,1]{1,0:T(1,128)}, bf16[8,16,1792]{2,1,0:T(8,128)(2,1)}) custom-call(bf16[2,2,2,16,2304]{4,3,2,1,0:T(8,128)(2,1)} %bitcast.4, bf16[512,2304]{1,0:T(8,128)(2,1)} %te.1, bf16[2,2,2,16,1792]{4,3,2,1,0:T(8,128)(2,1)} %bitcast.5, bf16[512,1792]{1,0:T(8,128)(2,1)} %se.1, s32[512]{0:T(512)} %lab.1, s32[512]{0:T(512)} %msk.1), custom_call_target="tpu_custom_call" | custom-call | tf_op jit(solution)/shard_map/distill/pallas_call | solution.py:410
  92.5 1.8 %copy.11 = bf16[128,1792]{1,0:T(8,128)(2,1)} copy(bf16[128,1792]{1,0:T(8,128)(2,1)} %bitcast.6) | data formatting | bytes 917504
